TPU v7x, 768 devices: a whole 4x8x12 slice. The times are simulated.
768 devices in a mesh: grp: 24 (over z, core), peer: 32 (over y, x).
Axes of the slice: x: 4, y: 8, z: 12, core: 2. Of those that a mesh axis runs over, the one named last changes fastest.
Arguments:
- grads: bfloat16 [393216, 512], P(('grp', 'peer')), may hold values from -1.796875 to 1.796875
- send_slot: int32 [768, 512], P(('grp', 'peer')), may hold values from 0 to 1535, as said below
- recv_row: int32 [768, 1536], P(('grp', 'peer')), may hold values from 0 to 768, as said below
- table: float32 [589824, 512], P(('grp', 'peer')), may hold values from -1.2 to 1.2
- accum: float32 [589824], P(('grp', 'peer')), may hold values from 0.05 to 2
Outputs:
- new_table: float32 [589824, 512], P(('grp', 'peer'))
- new_accum: float32 [589824], P(('grp', 'peer'))
- returned: bfloat16 [393216, 512], P(('grp', 'peer'))
Inputs may be any that keep to these rules, and one draw needn't show every extreme that they name: Within one device the slots are distinct; send_slot // 2 is the owning device's index over grp+peer. Some 64 owners receive 2 rows from every device. recv_row[o, s * 2 + c] is the local row of owner o updated by the row that device s placed in slot o * 2 + c, and equals 768 exactly where device s placed no row there. Rows from one device to one owner are distinct; different devices may name the same row.
All inputs are finite; a program needn't handle non-finite values.
Results may differ from a plain program's by a relative error of at most 0.001.
Values may be sent and summed in bfloat16 or wider, within the bound.
A program may use at most 32 MiB of HBM per device.

v0:
```python
import jax
import jax.numpy as jnp
from jax import lax
from jax.sharding import PartitionSpec as P

LEARN_RATE = 0.1
EPSILON = 1e-08


def per_device(grads, send_slot, recv_row, table, accum):
    n_grp = lax.axis_size("grp")
    n_peer = lax.axis_size("peer")
    slot_count = recv_row.shape[1]
    slot_cap = slot_count // (n_grp * n_peer)
    width = grads.shape[1]
    row_count = table.shape[0]
    my_slots = send_slot[0]
    outgoing = jnp.zeros((slot_count, width), jnp.bfloat16).at[my_slots].set(grads)
    outgoing = outgoing.reshape(n_grp, n_peer, slot_cap, width)
    arrived = lax.all_to_all(
        lax.all_to_all(outgoing, "grp", split_axis=0, concat_axis=0, tiled=True),
        "peer",
        split_axis=1,
        concat_axis=1,
        tiled=True,
    )
    arrived = arrived.reshape(slot_count, width)
    row_ids = recv_row[0]
    selector = (jnp.arange(row_count, dtype=jnp.int32)[:, None] == row_ids[None, :]).astype(
        jnp.bfloat16
    )
    summed = jnp.dot(selector, arrived, preferred_element_type=jnp.float32)
    new_accum = accum + jnp.mean(summed * summed, axis=1)
    new_table = table - LEARN_RATE * summed / (jnp.sqrt(new_accum) + EPSILON)[:, None]
    padded = jnp.concatenate(
        [new_table.astype(jnp.bfloat16), jnp.zeros((1, width), jnp.bfloat16)], axis=0
    )
    answers = padded[row_ids].reshape(n_grp, n_peer, slot_cap, width)
    answers = lax.all_to_all(
        lax.all_to_all(answers, "grp", split_axis=0, concat_axis=0, tiled=True),
        "peer",
        split_axis=1,
        concat_axis=1,
        tiled=True,
    )
    returned = answers.reshape(slot_count, width)[my_slots]
    return (new_table, new_accum, returned)


def solution(mesh):
    return jax.shard_map(
        per_device,
        mesh=mesh,
        in_specs=(
            P(("grp", "peer"), None),
            P(("grp", "peer"), None),
            P(("grp", "peer"), None),
            P(("grp", "peer"), None),
            P(("grp", "peer")),
        ),
        out_specs=(P(("grp", "peer"), None), P(("grp", "peer")), P(("grp", "peer"), None)),
        check_vma=False,
    )
```

profile of v0, /device:TPU:1, one launch (start us, length us, event | category | flops | bytes accessed | tf_op | source)
XLA Modules:
  0.0 251.6 jit_solution(13536458766361230911)
XLA Ops:
  0.6 0.7 compare_select_fusion.1
  1.3 3.4 %scatter_custom_fusion = bf16[1536,512]{1,0:T(8,128)(2,1)S(1)} fusion(s32[512]{0:T(512)S(1)} %bitcast.6, bf16[512,512]{1,0:T(8,128)(2,1)} %param.5, bf16[]{:T(256)} %constant.8.clone.1), kind=kCustom, calls=%fused_computation.8 | custom fusion | bytes 1573376 | tf_op jit(solution)/shard_map/scatter | solution.py:18
  4.8 0.6 reshape.75
  5.4 72.4 %all_to_all.20 = bf16[24,32,2,512]{3,2,1,0:T(2,128)(2,1)S(1)} all-to-all(bf16[24,32,2,512]{3,2,1,0:T(2,128)(2,1)S(1)} %reshape.75), channel_id=1, replica_groups=mesh['grp'=24,'peer'=32] {'grp'}, dimensions={0} | all-to-all | bytes 3145728 | tf_op jit(solution)/shard_map/all_to_all | solution.py:21
  77.8 2.8 %copy.15 = bf16[24,32,2,512]{3,2,0,1:T(2,128)(2,1)} copy(bf16[24,32,2,512]{3,2,1,0:T(2,128)(2,1)S(1)} %all_to_all.20) | data formatting | bytes 3145728 | tf_op jit(solution)/shard_map/all_to_all | solution.py:21
  80.7 9.8 %all-to-all-start.1 = ((bf16[24,32,2,512]{3,2,0,1:T(2,128)(2,1)}), bf16[24,32,2,512]{3,2,0,1:T(2,128)(2,1)S(1)}, u32[]{:S(2)}, u32[]{:S(2)}) async-start(bf16[24,32,2,512]{3,2,0,1:T(2,128)(2,1)} %copy.15), calls=%async_computation.1 | async-start | bytes 3145728 | tf_op jit(solution)/shard_map/all_to_all | solution.py:20
  90.5 35.2 %all-to-all-done.1 = bf16[24,32,2,512]{3,2,0,1:T(2,128)(2,1)S(1)} async-done(((bf16[24,32,2,512]{3,2,0,1:T(2,128)(2,1)}), bf16[24,32,2,512]{3,2,0,1:T(2,128)(2,1)S(1)}, u32[]{:S(2)}, u32[]{:S(2)}) %all-to-all-start.1) | async-done | bytes 1572896 | tf_op jit(solution)/shard_map/all_to_all | solution.py:20
  125.7 1.5 copy.16
  127.2 0.6 reshape.76
  127.9 0.0 copy-start.2
  127.9 0.0 copy-start
  127.9 1.5 multiply_reduce_fusion
  129.4 0.6 sqrt_add_fusion
  130.0 1.5 fusion.5
  131.5 0.1 concatenate.3
  131.6 4.8 %gather_fusion = bf16[1536,512]{1,0:T(8,128)(2,1)S(1)} fusion(bf16[769,512]{1,0:T(8,128)(2,1)S(1)} %concatenate.3, s32[2048]{0:T(1024)S(1)} %pad_clamp_fusion), kind=kCustom, calls=%fused_computation | custom fusion | bytes 3151872 | tf_op jit(solution)/shard_map/gather | solution.py:38
  136.4 0.6 reshape.77
  137.0 66.6 %all_to_all.21 = bf16[24,32,2,512]{3,2,1,0:T(2,128)(2,1)S(1)} all-to-all(bf16[24,32,2,512]{3,2,1,0:T(2,128)(2,1)S(1)} %reshape.77), channel_id=1, replica_groups=mesh['grp'=24,'peer'=32] {'grp'}, dimensions={0} | all-to-all | bytes 3145728 | tf_op jit(solution)/shard_map/all_to_all | solution.py:40
  203.6 2.8 %copy.17 = bf16[24,32,2,512]{3,2,0,1:T(2,128)(2,1)} copy(bf16[24,32,2,512]{3,2,1,0:T(2,128)(2,1)S(1)} %all_to_all.21) | data formatting | bytes 3145728 | tf_op jit(solution)/shard_map/all_to_all | solution.py:40
  206.4 5.1 %all-to-all-start.3 = ((bf16[24,32,2,512]{3,2,0,1:T(2,128)(2,1)}), bf16[24,32,2,512]{3,2,0,1:T(2,128)(2,1)S(1)}, u32[]{:S(2)}, u32[]{:S(2)}) async-start(bf16[24,32,2,512]{3,2,0,1:T(2,128)(2,1)} %copy.17), calls=%async_computation.3 | async-start | bytes 3145728 | tf_op jit(solution)/shard_map/all_to_all | solution.py:39
  211.6 35.2 %all-to-all-done.3 = bf16[24,32,2,512]{3,2,0,1:T(2,128)(2,1)S(1)} async-done(((bf16[24,32,2,512]{3,2,0,1:T(2,128)(2,1)}), bf16[24,32,2,512]{3,2,0,1:T(2,128)(2,1)S(1)}, u32[]{:S(2)}, u32[]{:S(2)}) %all-to-all-start.3) | async-done | bytes 1572896 | tf_op jit(solution)/shard_map/all_to_all | solution.py:39
  246.8 1.5 copy.18
  248.4 0.6 reshape.78
  249.0 2.6 %gather_fusion.1 = bf16[512,512]{1,0:T(8,128)(2,1)} fusion(bf16[1536,512]{1,0:T(8,128)(2,1)S(1)} %reshape.78, s32[1024]{0:T(1024)S(1)} %pad_clamp_fusion.1), kind=kCustom, calls=%fused_computation.1 | custom fusion | bytes 1050624 | tf_op jit(solution)/shard_map/gather | solution.py:46
  (8 shorter events, 0.1 us)
Async XLA Ops:
  80.7 9.8 %copy-start.1 = (s32[1,1536]{1,0:T(1,128)S(1)}, s32[1,1536]{1,0:T(1,128)}, u32[]{:S(2)}) copy-start(s32[1,1536]{1,0:T(1,128)} %param.7) | copy-start | bytes 18436
  80.7 45.0 %all-to-all-start.1 = ((bf16[24,32,2,512]{3,2,0,1:T(2,128)(2,1)}), bf16[24,32,2,512]{3,2,0,1:T(2,128)(2,1)S(1)}, u32[]{:S(2)}, u32[]{:S(2)}) async-start(bf16[24,32,2,512]{3,2,0,1:T(2,128)(2,1)} %copy.15), calls=%async_computation.1 | async-start | bytes 3145728 | tf_op jit(solution)/shard_map/all_to_all | solution.py:20
  127.9 1.5 copy-start.2
  127.9 2.1 copy-start
  206.4 40.4 %all-to-all-start.3 = ((bf16[24,32,2,512]{3,2,0,1:T(2,128)(2,1)}), bf16[24,32,2,512]{3,2,0,1:T(2,128)(2,1)S(1)}, u32[]{:S(2)}, u32[]{:S(2)}) async-start(bf16[24,32,2,512]{3,2,0,1:T(2,128)(2,1)} %copy.17), calls=%async_computation.3 | async-start | bytes 3145728 | tf_op jit(solution)/shard_map/all_to_all | solution.py:39
where the time goes:
time: 256 us; the launch traced here: 252 us
  blocking collectives  139 us (54%)
  waiting for transfers between devices  70.4 us (28%)
  local copies, waits for them, and re-layouts  22.2 us (9%)
  starting transfers between devices  14.9 us (6%)
  other arithmetic  2.84 us (1%)
    all_to_all x1, blocking collectives, per_device(): lax.all_to_all(outgoing, 'grp', split_axis=0, concat_axis=0, tiled=True)  72.4 us
    all_to_all x1, blocking collectives, per_device(): lax.all_to_all(answers, 'grp', split_axis=0, concat_axis=0, tiled=True)  66.6 us
    all_to_all x1, waiting for transfers between devices, per_device(): lax.all_to_all(lax.all_to_all(answers, 'grp', split_axis=0, concat_axis=0...  35.2 us
    all_to_all x1, waiting for transfers between devices, per_device(): lax.all_to_all(lax.all_to_all(outgoing, 'grp', split_axis=0, concat_axis=...  35.2 us
    all_to_all x1, starting transfers between devices, per_device(): lax.all_to_all(lax.all_to_all(outgoing, 'grp', split_axis=0, concat_axis=...  9.8 us
    all_to_all x1, starting transfers between devices, per_device(): lax.all_to_all(lax.all_to_all(answers, 'grp', split_axis=0, concat_axis=0...  5.14 us
  transfers between devices with their start and end apart: 2, of which 2 were waited for; matrix products, arithmetic and copies ran while one was open for 0% of the time, Pallas kernels for 0%

commit v1 on v0

v1 whole, which is shorter than its diff:
```python
import functools

import jax
import jax.numpy as jnp
from jax import lax
from jax.experimental import pallas as pl
from jax.experimental.pallas import tpu as pltpu
from jax.sharding import PartitionSpec as P

LEARN_RATE = 0.1
EPSILON = 1e-08
MESH = pl.DeviceIdType.MESH
CORES = 2


def update_kernel(
    n_grp, n_peer,
    grads, slot_row, slot_col, recv_row, recv_col, table, accum,
    new_table, new_accum, returned,
    out, arrived, answers, back, total, fresh, send_sem, recv_sem, send2_sem, recv2_sem, ready_sem,
):
    grp, peer = lax.axis_index("grp"), lax.axis_index("peer")
    n_z = n_grp // CORES
    z, core = grp // CORES, lax.rem(grp, CORES)
    me = grp * n_peer + peer
    plane = CORES * n_peer
    here = core * n_peer + peer
    slots = 2 * plane
    rows, width = table.shape
    count = grads.shape[0]

    barrier = pltpu.get_barrier_semaphore()

    def greet_grp(i, carry):
        pl.semaphore_signal(
            barrier, inc=1, device_id=(lax.rem(grp + i, n_grp), peer), device_id_type=MESH
        )
        return carry

    def greet_peer(i, carry):
        pl.semaphore_signal(
            barrier, inc=1, device_id=(grp, lax.rem(peer + i, n_peer)), device_id_type=MESH
        )
        return carry

    def confirm_peer(i, carry):
        pl.semaphore_signal(
            ready_sem, inc=1, device_id=(grp, lax.rem(peer + i, n_peer)), device_id_type=MESH
        )
        return carry

    lax.fori_loop(1, n_grp, greet_grp, 0)
    lax.fori_loop(1, n_peer, greet_peer, 0)
    pl.semaphore_wait(barrier, n_grp + n_peer - 2)
    lax.fori_loop(1, n_peer, confirm_peer, 0)
    pl.semaphore_wait(ready_sem, n_peer - 1)

    half = n_z // 2

    def far(step):
        return n_z - step if step else half

    def planes_to(step):
        return lax.rem(z + step, n_z), lax.rem(z + far(step), n_z)

    def planes_from(step):
        return lax.rem(z + n_z - step, n_z), lax.rem(z + n_z - far(step), n_z)

    def send(src, dst, to, s_sem, r_sem, i):
        spot = lax.rem(here + i, plane)
        pltpu.make_async_remote_copy(
            src_ref=src.at[to * plane + spot],
            dst_ref=dst.at[me],
            send_sem=s_sem,
            recv_sem=r_sem,
            device_id=(to * CORES + spot // n_peer, lax.rem(spot, n_peer)),
            device_id_type=MESH,
        ).start()

    def exchange(step, build, src, dst, s_sem, r_sems):
        first, second = planes_to(step)
        for to in (first, second):
            src[pl.ds(to * plane, plane)] = build(to).astype(jnp.bfloat16).reshape(plane, 2, width)
        sem_a, sem_b = r_sems.at[2 * step], r_sems.at[2 * step + 1]

        def both(i, carry):
            send(src, dst, first, s_sem, sem_a, i)
            send(src, dst, second, s_sem, sem_b, i)
            return carry

        if step == 0:
            pltpu.make_async_copy(src.at[me], dst.at[me], sem_a).start()
        else:
            send(src, dst, first, s_sem, sem_a, 0)
        send(src, dst, second, s_sem, sem_b, 0)
        lax.fori_loop(1, plane, both, 0)

    def collect(step, use, dst, r_sems):
        for k, src_z in enumerate(planes_from(step)):
            block = dst.at[pl.ds(src_z * plane, plane)]
            pltpu.make_async_copy(block, block, r_sems.at[2 * step + k]).wait()
            use(src_z, block[...].reshape(slots, width))

    def build_out(to):
        spot = lax.broadcasted_iota(jnp.int32, (slots, count), 0) + to * slots
        pick = (spot == slot_row[...]).astype(jnp.bfloat16)
        return jnp.dot(pick, grads[...], preferred_element_type=jnp.float32)

    for step in range(half):
        exchange(step, build_out, out, arrived, send_sem, recv_sem)

    total[...] = jnp.zeros_like(total)

    def add_block(src_z, block):
        ids = recv_row[:, pl.ds(pl.multiple_of(src_z * slots, slots), slots)]
        pick = (lax.broadcasted_iota(jnp.int32, (rows, slots), 0) == ids).astype(jnp.bfloat16)
        total[...] += jnp.dot(pick, block, preferred_element_type=jnp.float32)

    for step in range(half):
        collect(step, add_block, arrived, recv_sem)

    gsum = total[...]
    fresh_accum = accum[...] + jnp.sum(gsum * gsum, axis=1, keepdims=True) * (1.0 / width)
    new_accum[...] = fresh_accum
    updated = table[...] - LEARN_RATE * gsum / (jnp.sqrt(fresh_accum) + EPSILON)
    new_table[...] = updated
    fresh[...] = updated.astype(jnp.bfloat16)

    def build_back(to):
        ids = recv_col[pl.ds(pl.multiple_of(to * slots, slots), slots), :]
        pick = (lax.broadcasted_iota(jnp.int32, (slots, rows), 1) == ids).astype(jnp.bfloat16)
        return jnp.dot(pick, fresh[...], preferred_element_type=jnp.float32)

    for step in range(half):
        exchange(step, build_back, answers, back, send2_sem, recv2_sem)

    total[pl.ds(0, count), :] = jnp.zeros((count, width), jnp.float32)

    def place_block(src_z, block):
        spot = lax.broadcasted_iota(jnp.int32, (count, slots), 1) + src_z * slots
        pick = (spot == slot_col[...]).astype(jnp.bfloat16)
        total[pl.ds(0, count), :] += jnp.dot(pick, block, preferred_element_type=jnp.float32)

    for step in range(half):
        collect(step, place_block, back, recv2_sem)
    returned[...] = total[pl.ds(0, count), :].astype(jnp.bfloat16)

    others = n_grp * n_peer - 1
    for src, sem in ((out, send_sem), (answers, send2_sem)):
        sent = src.at[pl.ds(0, others)]
        pltpu.make_async_copy(sent, sent, sem).wait()


def per_device(grads, send_slot, recv_row, table, accum):
    n_grp, n_peer = lax.axis_size("grp"), lax.axis_size("peer")
    devices = n_grp * n_peer
    count, width = grads.shape
    rows = table.shape[0]
    slot_count = recv_row.shape[1]
    vmem = pl.BlockSpec(memory_space=pltpu.VMEM)
    blocks = pltpu.VMEM((devices, 2, width), jnp.bfloat16)
    n_z = n_grp // CORES
    new_table, new_accum, returned = pl.pallas_call(
        functools.partial(update_kernel, n_grp, n_peer),
        out_shape=(
            jax.ShapeDtypeStruct((rows, width), jnp.float32),
            jax.ShapeDtypeStruct((rows, 1), jnp.float32),
            jax.ShapeDtypeStruct((count, width), jnp.bfloat16),
        ),
        in_specs=[vmem] * 7,
        out_specs=(vmem, vmem, vmem),
        scratch_shapes=[
            blocks, blocks, blocks, blocks,
            pltpu.VMEM((rows, width), jnp.float32),
            pltpu.VMEM((rows, width), jnp.bfloat16),
            pltpu.SemaphoreType.DMA,
            pltpu.SemaphoreType.DMA((n_z,)),
            pltpu.SemaphoreType.DMA,
            pltpu.SemaphoreType.DMA((n_z,)),
            pltpu.SemaphoreType.REGULAR,
        ],
        compiler_params=pltpu.CompilerParams(
            collective_id=0, has_side_effects=True, vmem_limit_bytes=48 * 2**20
        ),
    )(
        grads, send_slot, send_slot.reshape(count, 1), recv_row,
        recv_row.reshape(slot_count, 1), table, accum.reshape(rows, 1),
    )
    return new_table, new_accum.reshape(rows), returned


def solution(mesh):
    rows = P(("grp", "peer"), None)
    return jax.shard_map(
        per_device,
        mesh=mesh,
        in_specs=(rows, rows, rows, rows, P(("grp", "peer"))),
        out_specs=(rows, P(("grp", "peer")), rows),
        check_vma=False,
    )
```

time: 256 us -> 155 us (0.61); the launches traced: 252 us -> 154 us
  Pallas kernels: 0 us -> 143 us
  blocking collectives: 139 us -> 0 us
  waiting for transfers between devices: 70.4 us -> 0 us
  starting transfers between devices: 14.9 us -> 0 us
  local copies, waits for them, and re-layouts: 22.2 us -> 9.21 us
    pallas_call x0 -> x1, Pallas kernels: none -> 143 us  [per_device(): pl.pallas_call(functools.partial(update_kernel, n_grp, n_peer), out_shape...]
    all_to_all x2 -> x0, blocking collectives: 139 us -> none  [the longest x1 72.4 us: per_device(): lax.all_to_all(outgoing, 'grp', split_axis=0, concat_axis=0, tiled=True)]
    all_to_all x2 -> x0, waiting for transfers between devices: 70.4 us -> none  [the longest x1 35.2 us: per_device(): lax.all_to_all(lax.all_to_all(answers, 'grp', split_axis=0, concat_axis=0...]
    all_to_all x2 -> x0, starting transfers between devices: 14.9 us -> none  [the longest x1 9.8 us: per_device(): lax.all_to_all(lax.all_to_all(outgoing, 'grp', split_axis=0, concat_axis=...]
    all_to_all x4 -> x0, local copies, waits for them, and re-layouts: 8.72 us -> none  [the longest x1 2.82 us: per_device(): lax.all_to_all(answers, 'grp', split_axis=0, concat_axis=0, tiled=True)]
    gather x2 -> x0, local copies, waits for them, and re-layouts: 7.44 us -> none  [the longest x1 4.81 us: per_device(): answers = padded[row_ids].reshape(n_grp, n_peer, slot_cap, width)]
    unnamed x6 -> x16, local copies, waits for them, and re-layouts: 0.02 us -> 6.5 us
    scatter x1 -> x0, local copies, waits for them, and re-layouts: 3.43 us -> none  [per_device(): jnp.zeros((slot_count, width), jnp.bfloat16).at[my_slots].set(grads)]
  transfers between devices with their start and end apart: 2 -> 0, of which waited for: 2 -> 0; matrix products, arithmetic and copies ran while one was open for 0% -> 0% of each run, Pallas kernels for 0% -> 0%
where the time goes in v1:
time: 155 us; the launch traced here: 154 us
  Pallas kernels  143 us (92%)
  local copies, waits for them, and re-layouts  9.21 us (6%)
  other arithmetic  1.76 us (1%)
    pallas_call x1, Pallas kernels, per_device(): pl.pallas_call(functools.partial(update_kernel, n_grp, n_peer), out_shape...  143 us
    unnamed x16, local copies, waits for them, and re-layouts  6.5 us

profile of v1, /device:TPU:1, one launch (start us, length us, event | category | flops | bytes accessed | tf_op | source)
XLA Modules:
  0.0 154.4 jit_solution(14780178273175492425)
XLA Ops:
  0.6 0.0 copy-start.1
  0.6 0.9 copy.8.slot_col
  1.5 0.8 reshape.22.accum
  2.4 1.0 copy.9.recv_col
  3.4 0.0 copy-done.1
  3.4 0.0 copy-start
  3.4 1.4 copy-done
  4.8 0.0 copy-start.5
  4.8 0.7 copy-done.5
  5.5 0.0 copy-start.6
  5.5 0.7 copy-done.6
  6.2 142.7 %shard_map.76 = (f32[768,512]{1,0:T(8,128)S(1)}, f32[768,1]{1,0:T(8,128)S(1)}, bf16[512,512]{1,0:T(8,128)(2,1)S(1)}) custom-call(bf16[512,512]{1,0:T(8,128)(2,1)S(1)} %copy-done.1, s32[1,512]{1,0:T(1,128)S(1)} %copy-done.6, s32[512,1]{1,0:T(8,128)S(1)} %copy.8.slot_col, s32[1,1536]{1,0:T(1,128)S(1)} %copy-done.5, s32[1536,1]{1,0:T(8,128)S(1)} %copy.9.recv_col, ...), custom_call_target="tpu_custom_call" | custom-call | tf_op jit(solution)/shard_map/pallas_call | solution.py:163
  148.9 0.0 copy-start.2
  148.9 0.8 copy-done.2
  149.7 0.0 copy-start.4
  149.7 0.7 copy-done.4
  150.4 1.8 %reduce = f32[768]{0:T(1024)} reduce(f32[768,1]{1,0:T(8,128)} %copy-done.4, f32[]{:T(128)} %constant.3), dimensions={1}, to_apply=%get-tuple-element.7.reduce_sub_computation | reduce | bytes 6148 | tf_op jit(solution)/shard_map/pallas_call | solution.py:163
  152.2 0.0 copy-start.3
  152.2 1.1 copy.13
  153.3 0.3 copy-done.3
  153.6 0.8 copy.14
Async XLA Ops:
  0.6 2.7 %copy-start.1 = (bf16[512,512]{1,0:T(8,128)(2,1)S(1)}, bf16[512,512]{1,0:T(8,128)(2,1)}, u32[]{:S(2)}) copy-start(bf16[512,512]{1,0:T(8,128)(2,1)} %grads.1) | copy-start | bytes 1572868
  3.4 1.4 copy-start
  4.8 0.7 copy-start.5
  5.5 0.7 copy-start.6
  148.9 0.8 copy-start.2
  149.7 0.7 copy-start.4
  152.2 1.4 copy-start.3

commit v2 on v0

v2 whole, which is shorter than its diff:
```python
import functools

import jax
import jax.numpy as jnp
from jax import lax
from jax.experimental import pallas as pl
from jax.experimental.pallas import tpu as pltpu
from jax.sharding import PartitionSpec as P

LEARN_RATE = 0.1
EPSILON = 1e-08
MESH = pl.DeviceIdType.MESH
CORES = 2
LANES = 128


def near_first(n_z):
    order = [0]
    for d in range(1, (n_z + 1) // 2):
        order += [d, n_z - d]
    return order + ([n_z // 2] if n_z % 2 == 0 else [])


def as_column(row, copies):
    return jnp.transpose(jnp.broadcast_to(row, (copies, row.shape[1])))


def update_kernel(
    n_grp, n_peer, cap,
    grads_hbm, slot_hbm, recv_hbm, table_hbm, accum_hbm,
    table_out, accum_out, returned_out, flag_out,
    grads, slot, recv, table, accum, key_row, key_col, returned,
    packed, packed_in, ids, ids_in, mid, arrived, answers, answers_in, repacked, repacked_in,
    flags, total, fresh,
    load_sem, send_sem, pack_sem, ids_sem, row_sem, flag_sem, answer_sem, back_sem, store_sem,
):
    grp, peer = lax.axis_index("grp"), lax.axis_index("peer")
    n_z = n_grp // CORES
    z, core = grp // CORES, lax.rem(grp, CORES)
    plane = CORES * n_peer
    here = core * n_peer + peer
    slots = 2 * plane
    rows, width = table.shape
    count = grads.shape[0]
    order = near_first(n_z)

    loads = [
        pltpu.make_async_copy(src, dst, load_sem.at[i])
        for i, (src, dst) in enumerate(
            ((slot_hbm, slot), (grads_hbm, grads), (recv_hbm, recv), (accum_hbm, accum), (table_hbm, table))
        )
    ]
    for load in loads:
        load.start()

    barrier = pltpu.get_barrier_semaphore()

    def at_place(spot):
        return (z * CORES + spot // n_peer, lax.rem(spot, n_peer))

    def greet_line(i, carry):
        there = lax.rem(z + i, n_z) * CORES + core
        pl.semaphore_signal(barrier, inc=1, device_id=(there, peer), device_id_type=MESH)
        return carry

    def greet_plane(i, carry):
        pl.semaphore_signal(
            barrier, inc=1, device_id=at_place(lax.rem(here + i, plane)), device_id_type=MESH
        )
        return carry

    lax.fori_loop(1, n_z, greet_line, 0)
    lax.fori_loop(1, plane, greet_plane, 0)

    loads[0].wait()
    goal = lax.div(slot[...], slots)
    member = (lax.broadcasted_iota(jnp.int32, (-(-n_z // 16) * 16, count), 0) == goal)
    before = lax.broadcasted_iota(jnp.int32, (count, count), 0) < lax.broadcasted_iota(
        jnp.int32, (count, count), 1
    )
    ranks = jnp.dot(
        member.astype(jnp.bfloat16), before.astype(jnp.bfloat16), preferred_element_type=jnp.float32
    )
    rank = jnp.sum(jnp.where(member, ranks, 0.0), axis=0, keepdims=True).astype(jnp.int32)
    key_row[...] = jnp.where(rank < cap, goal * LANES + rank, -1)
    key_col[...] = as_column(key_row[...], LANES)
    over = jnp.max(jnp.where(rank < cap, 0.0, 1.0), axis=1, keepdims=True)
    place = (slot[...] - goal * slots + 1).astype(jnp.float32).astype(jnp.bfloat16)
    place = jnp.broadcast_to(place, (16, count))
    last_lane = lax.broadcasted_iota(jnp.int32, (8, LANES), 1) == LANES - 1

    loads[1].wait()
    pl.semaphore_wait(barrier, n_z + plane - 2)

    def line_copy(src, dst, sem, to):
        return pltpu.make_async_remote_copy(
            src_ref=src, dst_ref=dst, send_sem=send_sem.at[0], recv_sem=sem,
            device_id=(to * CORES + core, peer), device_id_type=MESH,
        )

    for k in order:
        to = lax.rem(z + k, n_z)
        pick = lax.broadcasted_iota(jnp.int32, (LANES, count), 0) + to * LANES == key_row[...]
        pick = pick.astype(jnp.bfloat16)
        block = jnp.dot(pick[:cap], grads[...], preferred_element_type=jnp.float32)
        names = lax.dot_general(
            place, pick, (((1,), (1,)), ((), ())), preferred_element_type=jnp.float32
        )
        names = jnp.where(last_lane, over, names[:8])
        if k == 0:
            packed_in[0] = block.astype(jnp.bfloat16)
            ids_in[0] = names
        else:
            packed[k] = block.astype(jnp.bfloat16)
            ids[k] = names
            line_copy(packed.at[k], packed_in.at[k], pack_sem.at[k], to).start()
            line_copy(ids.at[k], ids_in.at[k], ids_sem.at[k], to).start()

    def spread_plane(src, dst, sem, k):
        def one(i, carry):
            spot = lax.rem(here + i, plane)
            pltpu.make_async_remote_copy(
                src_ref=src.at[k * plane + spot],
                dst_ref=dst.at[k * plane + here],
                send_sem=send_sem.at[1],
                recv_sem=sem.at[k],
                device_id=at_place(spot),
                device_id_type=MESH,
            ).start()
            return carry

        mine = k * plane + here
        pltpu.make_async_copy(src.at[mine], dst.at[mine], sem.at[k]).start()
        lax.fori_loop(1, plane, one, 0)

    def wait_plane(dst, sem, k):
        block = dst.at[pl.ds(k * plane, plane)]
        pltpu.make_async_copy(block, block, sem.at[k]).wait()
        return block[...].reshape(slots, width)

    def unpack_matrix(k):
        spot = lax.broadcasted_iota(jnp.int32, (slots, LANES), 0) + 1
        return (spot.astype(jnp.float32) == ids_in[k][0:1, :]).astype(jnp.bfloat16)

    def origin(k):
        return lax.rem(z + n_z - k, n_z)

    loads[2].wait()
    total[...] = jnp.zeros_like(total)

    def add_rows(k):
        block = wait_plane(arrived, row_sem, k)
        names = recv[:, pl.ds(pl.multiple_of(origin(k) * slots, slots), slots)]
        pick = (lax.broadcasted_iota(jnp.int32, (rows, slots), 0) == names).astype(jnp.bfloat16)
        total[...] += jnp.dot(pick, block, preferred_element_type=jnp.float32)

    lag = 2
    for i in range(n_z + lag):
        if i < n_z:
            k = order[i]
            if k:
                pltpu.make_async_copy(packed_in.at[k], packed_in.at[k], pack_sem.at[k]).wait()
                pltpu.make_async_copy(ids_in.at[k], ids_in.at[k], ids_sem.at[k]).wait()
            block = jnp.dot(
                unpack_matrix(k)[:, :cap], packed_in[k], preferred_element_type=jnp.float32
            )
            mid[pl.ds(k * plane, plane)] = block.astype(jnp.bfloat16).reshape(plane, 2, width)
            spread_plane(mid, arrived, row_sem, k)
        if i >= lag:
            add_rows(order[i - lag])

    some = jnp.max(ids_in[...], axis=0)
    some = jnp.max(jnp.where(last_lane, some, 0.0), axis=1, keepdims=True)
    flags[pl.ds(here, 1)] = jnp.broadcast_to(some, (1, 8, LANES))

    def tell(i, carry):
        pltpu.make_async_remote_copy(
            src_ref=flags.at[here], dst_ref=flags.at[here], send_sem=send_sem.at[2],
            recv_sem=flag_sem, device_id=at_place(lax.rem(here + i, plane)), device_id_type=MESH,
        ).start()
        return carry

    lax.fori_loop(1, plane, tell, 0)

    loads[3].wait()
    loads[4].wait()
    gsum = total[...]
    fresh_accum = as_column(accum[...], LANES)[:, :1] + jnp.sum(
        gsum * gsum, axis=1, keepdims=True
    ) * (1.0 / width)
    updated = table[...] - LEARN_RATE * gsum / (jnp.sqrt(fresh_accum) + EPSILON)
    fresh[...] = updated.astype(jnp.bfloat16)

    far = order[::-1]
    for i in range(n_z + lag):
        if i < n_z:
            k = far[i]
            names = recv[:, pl.ds(pl.multiple_of(origin(k) * slots, slots), slots)]
            names = as_column(names, LANES)[:, :1]
            pick = (lax.broadcasted_iota(jnp.int32, (slots, rows), 1) == names).astype(jnp.bfloat16)
            block = jnp.dot(pick, fresh[...], preferred_element_type=jnp.float32)
            answers[pl.ds(k * plane, plane)] = block.astype(jnp.bfloat16).reshape(plane, 2, width)
            spread_plane(answers, answers_in, answer_sem, k)
        if i == 0:
            table[...] = updated
            accum[...] = jnp.transpose(jnp.broadcast_to(fresh_accum, (rows, LANES)))[:1, :]
            stores = [
                pltpu.make_async_copy(table, table_out, store_sem.at[0]),
                pltpu.make_async_copy(accum, accum_out, store_sem.at[1]),
            ]
            for store in stores:
                store.start()
        if i >= lag:
            k = far[i - lag]
            block = wait_plane(answers_in, answer_sem, k)
            block = lax.dot_general(
                unpack_matrix(k), block, (((0,), (0,)), ((), ())), preferred_element_type=jnp.float32
            )
            if k == 0:
                repacked_in[0] = block[:cap].astype(jnp.bfloat16)
            else:
                repacked[k] = block[:cap].astype(jnp.bfloat16)
                line_copy(repacked.at[k], repacked_in.at[k], back_sem.at[k], origin(k)).start()

    total[pl.ds(0, count), :] = jnp.zeros((count, width), jnp.float32)
    for k in far:
        if k:
            pltpu.make_async_copy(repacked_in.at[k], repacked_in.at[k], back_sem.at[k]).wait()
        lane = lax.broadcasted_iota(jnp.int32, (count, LANES), 1) + lax.rem(z + k, n_z) * LANES
        pick = (lane == key_col[...]).astype(jnp.bfloat16)[:, :cap]
        total[pl.ds(0, count), :] += jnp.dot(
            pick, repacked_in[k], preferred_element_type=jnp.float32
        )
    returned[...] = total[pl.ds(0, count), :].astype(jnp.bfloat16)
    stores.append(pltpu.make_async_copy(returned, returned_out, store_sem.at[2]))
    stores[-1].start()

    told = flags.at[pl.ds(0, plane - 1)]
    pltpu.make_async_copy(told, told, flag_sem).wait()
    flag_out[...] = jnp.max(flags[...], axis=0)

    for k in range(1, n_z):
        for part in (packed, ids, repacked):
            pltpu.make_async_copy(part.at[k], part.at[k], send_sem.at[0]).wait()
    for part in (mid, answers):
        sent = part.at[pl.ds(0, n_z * (plane - 1))]
        pltpu.make_async_copy(sent, sent, send_sem.at[1]).wait()
    pltpu.make_async_copy(told, told, send_sem.at[2]).wait()
    for store in stores:
        store.wait()


def slow_update(grads, send_slot, recv_row, table, accum):
    n_grp, n_peer = lax.axis_size("grp"), lax.axis_size("peer")
    slot_count, width, row_count = recv_row.shape[1], grads.shape[1], table.shape[0]
    slot_cap = slot_count // (n_grp * n_peer)
    my_slots, row_ids = send_slot[0], recv_row[0]

    def exchange(blocks):
        blocks = blocks.reshape(n_grp, n_peer, slot_cap, width)
        blocks = lax.all_to_all(blocks, "grp", split_axis=0, concat_axis=0, tiled=True)
        blocks = lax.all_to_all(blocks, "peer", split_axis=1, concat_axis=1, tiled=True)
        return blocks.reshape(slot_count, width)

    arrived = exchange(jnp.zeros((slot_count, width), jnp.bfloat16).at[my_slots].set(grads))
    selector = jnp.arange(row_count, dtype=jnp.int32)[:, None] == row_ids[None, :]
    summed = jnp.dot(selector.astype(jnp.bfloat16), arrived, preferred_element_type=jnp.float32)
    new_accum = accum + jnp.mean(summed * summed, axis=1)
    new_table = table - LEARN_RATE * summed / (jnp.sqrt(new_accum) + EPSILON)[:, None]
    padded = jnp.concatenate(
        [new_table.astype(jnp.bfloat16), jnp.zeros((1, width), jnp.bfloat16)], axis=0
    )
    return new_table, new_accum, exchange(padded[row_ids])[my_slots]


def per_device(grads, send_slot, recv_row, table, accum):
    n_grp, n_peer = lax.axis_size("grp"), lax.axis_size("peer")
    count, width = grads.shape
    rows = table.shape[0]
    slot_count = recv_row.shape[1]
    devices = n_grp * n_peer
    n_z, plane = n_grp // CORES, CORES * n_peer
    slots = 2 * plane
    cap = slots * 5 // 8
    hbm = pl.BlockSpec(memory_space=pltpu.HBM)
    vmem = pl.BlockSpec(memory_space=pltpu.VMEM)
    blocks = pltpu.VMEM((devices, 2, width), jnp.bfloat16)
    packs = pltpu.VMEM((n_z, cap, width), jnp.bfloat16)
    names = pltpu.VMEM((n_z, 8, LANES), jnp.float32)
    dma = pltpu.SemaphoreType.DMA
    new_table, new_accum, returned, flag = pl.pallas_call(
        functools.partial(update_kernel, n_grp, n_peer, cap),
        out_shape=(
            jax.ShapeDtypeStruct((rows, width), jnp.float32),
            jax.ShapeDtypeStruct((1, rows), jnp.float32),
            jax.ShapeDtypeStruct((count, width), jnp.bfloat16),
            jax.ShapeDtypeStruct((8, LANES), jnp.float32),
        ),
        in_specs=[hbm] * 5,
        out_specs=(hbm, hbm, hbm, vmem),
        scratch_shapes=[
            pltpu.VMEM((count, width), jnp.bfloat16),
            pltpu.VMEM((1, count), jnp.int32),
            pltpu.VMEM((1, slot_count), jnp.int32),
            pltpu.VMEM((rows, width), jnp.float32),
            pltpu.VMEM((1, rows), jnp.float32),
            pltpu.VMEM((1, count), jnp.int32),
            pltpu.VMEM((count, LANES), jnp.int32),
            pltpu.VMEM((count, width), jnp.bfloat16),
            packs, packs, names, names, blocks, blocks, blocks, blocks, packs, packs,
            pltpu.VMEM((plane, 8, LANES), jnp.float32),
            pltpu.VMEM((rows, width), jnp.float32),
            pltpu.VMEM((rows, width), jnp.bfloat16),
            dma((5,)), dma((3,)), dma((n_z,)), dma((n_z,)), dma((n_z,)), dma, dma((n_z,)), dma((n_z,)),
            dma((3,)),
        ],
        compiler_params=pltpu.CompilerParams(
            collective_id=0, has_side_effects=True, vmem_limit_bytes=48 * 2**20
        ),
    )(grads, send_slot, recv_row, table, accum.reshape(1, rows))
    fast = (new_table, new_accum.reshape(rows), returned)
    return lax.cond(
        flag[0, 0] > 0.5,
        lambda fast, *args: slow_update(*args),
        lambda fast, *args: fast,
        fast, grads, send_slot, recv_row, table, accum,
    )


def solution(mesh):
    rows = P(("grp", "peer"), None)
    return jax.shard_map(
        per_device,
        mesh=mesh,
        in_specs=(rows, rows, rows, rows, P(("grp", "peer"))),
        out_specs=(rows, P(("grp", "peer")), rows),
        check_vma=False,
    )
```

time: 256 us -> 127 us (0.50); the launches traced: 252 us -> 127 us
  blocking collectives: 139 us -> 0 us
  Pallas kernels: 0 us -> 120 us
  waiting for transfers between devices: 70.4 us -> 0 us
  local copies, waits for them, and re-layouts: 22.2 us -> 5.8 us
  starting transfers between devices: 14.9 us -> 0 us
  other arithmetic: 2.84 us -> 0.02 us
    all_to_all x2 -> x0, blocking collectives: 139 us -> none  [the longest x1 72.4 us: per_device(): lax.all_to_all(outgoing, 'grp', split_axis=0, concat_axis=0, tiled=True)]
    pallas_call x0 -> x1, Pallas kernels: none -> 120 us  [per_device(): pl.pallas_call(functools.partial(update_kernel, n_grp, n_peer, cap), out_...]
    all_to_all x2 -> x0, waiting for transfers between devices: 70.4 us -> none  [the longest x1 35.2 us: per_device(): lax.all_to_all(lax.all_to_all(answers, 'grp', split_axis=0, concat_axis=0...]
    all_to_all x2 -> x0, starting transfers between devices: 14.9 us -> none  [the longest x1 9.8 us: per_device(): lax.all_to_all(lax.all_to_all(outgoing, 'grp', split_axis=0, concat_axis=...]
    all_to_all x4 -> x0, local copies, waits for them, and re-layouts: 8.72 us -> none  [the longest x1 2.82 us: per_device(): lax.all_to_all(answers, 'grp', split_axis=0, concat_axis=0, tiled=True)]
    gather x2 -> x0, local copies, waits for them, and re-layouts: 7.44 us -> none  [the longest x1 4.81 us: per_device(): answers = padded[row_ids].reshape(n_grp, n_peer, slot_cap, width)]
    unnamed x6 -> x10, local copies, waits for them, and re-layouts: 0.02 us -> 4.56 us
    scatter x1 -> x0, local copies, waits for them, and re-layouts: 3.43 us -> none  [per_device(): jnp.zeros((slot_count, width), jnp.bfloat16).at[my_slots].set(grads)]
  transfers between devices with their start and end apart: 2 -> 0, of which waited for: 2 -> 0; matrix products, arithmetic and copies ran while one was open for 0% -> 0% of each run, Pallas kernels for 0% -> 0%
where the time goes in v2:
time: 127 us
  Pallas kernels  120 us (94%)
  local copies, waits for them, and re-layouts  5.8 us (5%)
  between operations  1.36 us (1%)
    pallas_call x1, Pallas kernels, per_device(): pl.pallas_call(functools.partial(update_kernel, n_grp, n_peer, cap), out_...  120 us
    unnamed x10, local copies, waits for them, and re-layouts  4.56 us

profile of v2, /device:TPU:1, one launch (start us, length us, event | category | flops | bytes accessed | tf_op | source)
XLA Modules:
  0.0 127.0 jit_solution(13015452842645320368)
XLA Ops:
  0.6 0.0 copy-start.2
  0.6 0.0 copy-start.3
  0.7 0.0 copy-start.1
  0.7 0.7 reshape.86.accum_hbm
  1.4 119.6 %shard_map.78 = (f32[768,512]{1,0:T(8,128)}, f32[1,768]{1,0:T(1,128)S(1)}, bf16[512,512]{1,0:T(8,128)(2,1)}, f32[8,128]{1,0:T(8,128)S(1)}) custom-call(bf16[512,512]{1,0:T(8,128)(2,1)} %grads_hbm.1, s32[1,512]{1,0:T(1,128)} %slot_hbm.1, s32[1,1536]{1,0:T(1,128)} %recv_hbm.1, f32[768,512]{1,0:T(8,128)} %table_hbm.1, f32[1,768]{1,0:T(1,128)S(1)} %reshape.86.accum_hbm), custom_call_target="tpu_custom_call" | custom-call | tf_op jit(solution)/shard_map/pallas_call | solution.py:291
  121.0 0.5 slice.3
  122.1 0.0 copy-done.2
  122.1 0.0 copy-done.3
  122.2 0.0 copy-done.1
  122.2 0.3 conditional.1
  122.4 0.0 copy-start.4
  122.4 2.7 %copy.28 = f32[768,512]{1,0:T(8,128)} copy(f32[768,512]{1,0:T(8,128)} %get-tuple-element.55) | data formatting | bytes 3145728
  125.1 0.0 copy-done.4
  125.1 1.9 %copy.29 = bf16[512,512]{1,0:T(8,128)(2,1)} copy(bf16[512,512]{1,0:T(8,128)(2,1)} %get-tuple-element.57) | data formatting | bytes 1048576
  (1 shorter events, 0.0 us)
Async XLA Ops:
  0.6 121.5 %copy-start.2 = (f32[768]{0:T(1024)S(1)}, f32[768]{0:T(1024)}, u32[]{:S(2)}) copy-start(f32[768]{0:T(1024)} %param.11) | copy-start | bytes 9220
  0.6 121.5 %copy-start.3 = (s32[1,512]{1,0:T(1,128)S(1)}, s32[1,512]{1,0:T(1,128)}, u32[]{:S(2)}) copy-start(s32[1,512]{1,0:T(1,128)} %slot_hbm.1) | copy-start | bytes 6148
  0.7 121.5 %copy-start.1 = (s32[1,1536]{1,0:T(1,128)S(1)}, s32[1,1536]{1,0:T(1,128)}, u32[]{:S(2)}) copy-start(s32[1,1536]{1,0:T(1,128)} %recv_hbm.1) | copy-start | bytes 18436
  122.4 2.7 %copy-start.4 = (f32[768]{0:T(1024)}, f32[768]{0:T(1024)S(1)}, u32[]{:S(2)}) copy-start(f32[768]{0:T(1024)S(1)} %get-tuple-element.56) | copy-start | bytes 9220
